TPU v7x, 128 devices: a whole 4x4x4 slice. The times are simulated.
128 devices in a mesh: head: 8 (over y, core), blk: 16 (over z, x).
Axes of the slice: x: 4, y: 4, z: 4, core: 2. Of those that a mesh axis runs over, the one named last changes fastest.
Arguments:
- tokens: bfloat16 [2, 8192, 2048], P(None, ('blk', 'head')), may hold values from -6 to 6
- cotangent: bfloat16 [2, 8192, 2048], P(None, ('blk', 'head')), may hold values from -6 to 6
- doc_lengths: int32 [2, 4], replicated, may hold values from 1 to 8189, as said below
- adapter_index: int32 [2, 1], replicated, may hold values from 0 to 1
- attn_gain: float32 [2048], replicated, may hold values from 0.25 to 1.75
- ffn_gain: float32 [2048], replicated, may hold values from 0.25 to 1.75
- w_qkv: bfloat16 [2048, 4096], P('blk', 'head'), may hold values from -0.125 to 0.125
- w_out: bfloat16 [2048, 2048], P('head', 'blk'), may hold values from -0.5 to 0.5
- w_gate: bfloat16 [2048, 8192], P('blk', 'head'), may hold values from -0.125 to 0.125
- w_up: bfloat16 [2048, 8192], P('blk', 'head'), may hold values from -0.125 to 0.125
- w_down: bfloat16 [8192, 2048], P('head', 'blk'), may hold values from -0.0625 to 0.0625
- qkv_in: bfloat16 [2, 2048, 16], replicated, may hold values from -0.125 to 0.125
- qkv_out: bfloat16 [2, 16, 4096], replicated, may hold values from -1 to 1
- attn_in: bfloat16 [2, 2048, 16], replicated, may hold values from -0.5 to 0.5
- attn_out: bfloat16 [2, 16, 2048], replicated, may hold values from -1 to 1
- gate_in: bfloat16 [2, 2048, 16], replicated, may hold values from -0.125 to 0.125
- gate_out: bfloat16 [2, 16, 8192], replicated, may hold values from -1 to 1
- up_in: bfloat16 [2, 2048, 16], replicated, may hold values from -0.125 to 0.125
- up_out: bfloat16 [2, 16, 8192], replicated, may hold values from -1 to 1
- down_in: bfloat16 [2, 8192, 16], replicated, may hold values from -0.0625 to 0.0625
- down_out: bfloat16 [2, 16, 2048], replicated, may hold values from -1 to 1
Outputs:
- result: float32 [2, 8192, 2048], P(None, ('blk', 'head'))
- input_grad: float32 [2, 8192, 2048], P(None, ('blk', 'head'))
- qkv_in_grad: float32 [2, 2048, 16], replicated
- qkv_out_grad: float32 [2, 16, 4096], replicated
- attn_in_grad: float32 [2, 2048, 16], replicated
- attn_out_grad: float32 [2, 16, 2048], replicated
- gate_in_grad: float32 [2, 2048, 16], replicated
- gate_out_grad: float32 [2, 16, 8192], replicated
- up_in_grad: float32 [2, 2048, 16], replicated
- up_out_grad: float32 [2, 16, 8192], replicated
- down_in_grad: float32 [2, 8192, 16], replicated
- down_out_grad: float32 [2, 16, 2048], replicated
Inputs may be any that keep to these rules, and one draw needn't show every extreme that they name: `doc_lengths`: each row sums to 8192. `adapter_index`: every adapter is named by some sequence.
All inputs are finite; a program needn't handle non-finite values.
Results may differ from a plain program's by a relative error of at most 0.025.
Values may be sent and summed in bfloat16 or wider, within the bound.
A program may use at most 192 MiB of HBM per device.

v0:
```python
from functools import partial

import jax
import jax.numpy as jnp
from jax import lax
from jax.experimental import pallas as pl
from jax.experimental.pallas import tpu as pltpu
from jax.sharding import PartitionSpec as P

MESH = pl.DeviceIdType.MESH
BF = jnp.bfloat16
F32 = jnp.float32
D = 2048
EXT = 128
CW = D + EXT
RANK = 16
WINDOW = 1024
EPS = 1e-05
THETA = 1000000.0
Y, CORES, Z, X = 4, 2, 4, 4
TOK = 64
SPAN = 512
SCALE = 128 ** (-0.5)
VMEM_BYTES = 66977792


def mm(a, b):
    return jnp.dot(a, b, preferred_element_type=F32)


def mm_nt(a, b):
    return lax.dot_general(a, b, (((1,), (1,)), ((), ())), preferred_element_type=F32)


def mm_tn(a, b):
    return lax.dot_general(a, b, (((0,), (0,)), ((), ())), preferred_element_type=F32)


class Place:
    def __init__(self):
        h = lax.axis_index("head")
        b = lax.axis_index("blk")
        self.h, self.b = h, b
        self.y, self.c = h // 2, h % 2
        self.z, self.x = b // 4, b % 4
        y, c, z, x = self.y, self.c, self.z, self.x
        self.yu, self.yd, self.yo = (y + 1) % 4, (y + 3) % 4, (y + 2) % 4
        self.xu, self.xd = (x + 1) % 4, (x + 3) % 4
        self.zu, self.zd = (z + 1) % 4, (z + 3) % 4
        self.sib = (y * 2 + (1 - c), b)
        self.yp, self.ym = (self.yu * 2 + c, b), (self.yd * 2 + c, b)
        self.xp, self.xm = (h, z * 4 + self.xu), (h, z * 4 + self.xd)
        self.zp, self.zm = (h, self.zu * 4 + x), (h, self.zd * 4 + x)
        self.next1, self.next2 = (h, (b + 1) % 16), (h, (b + 2) % 16)
        self.prev1, self.prev2 = (h, (b + 15) % 16), (h, (b + 14) % 16)

    def greet(self, peers):
        barrier = pltpu.get_barrier_semaphore()
        for peer in peers:
            pl.semaphore_signal(barrier, inc=1, device_id=peer, device_id_type=MESH)
        pl.semaphore_wait(barrier, len(peers))


class Net:
    def __init__(self, send, recv):
        self.send, self.recv, self.count, self.copies = send, recv, 0, []

    def push(self, src, dst, peer):
        i = self.count
        self.count += 1
        copy = pltpu.make_async_remote_copy(
            src_ref=src,
            dst_ref=dst,
            send_sem=self.send.at[i],
            recv_sem=self.recv.at[i],
            device_id=peer,
            device_id_type=MESH,
        )
        copy.start()
        self.copies.append(copy)
        return copy

    def settle(self, copies):
        for copy in copies:
            copy.wait_send()
            self.copies = [other for other in self.copies if other is not copy]

    def drain(self):
        self.settle(list(self.copies))


class Gather:
    def __init__(self, net, at, slot, extent):
        self.net, self.at, self.slot, self.half = net, at, slot, extent // 2
        own = slot(at.y, at.c)
        self.up = net.push(own, own, at.yp)
        self.down = net.push(own, own, at.ym)
        self.side = [net.push(own, own, at.sib)]

    def relay(self):
        at, net, half = self.at, self.net, self.half
        below = self.slot(at.yd, at.c)
        above = self.slot(at.yu, at.c)
        self.up.wait_recv()
        part = below.at[pl.ds(0, half)]
        self.far_a = net.push(part, part, at.yp)
        self.side.append(net.push(below, below, at.sib))
        self.down.wait_recv()
        part = above.at[pl.ds(half, half)]
        self.far_b = net.push(part, part, at.ym)
        self.side.append(net.push(above, above, at.sib))

    def last(self):
        at, net, half = self.at, self.net, self.half
        far = self.slot(at.yo, at.c)
        self.far_a.wait_recv()
        part = far.at[pl.ds(0, half)]
        self.side.append(net.push(part, part, at.sib))
        self.far_b.wait_recv()
        part = far.at[pl.ds(half, half)]
        self.side.append(net.push(part, part, at.sib))

    def done(self):
        for copy in self.side:
            copy.wait_recv()

    def settle(self):
        self.net.settle([self.up, self.down, self.far_a, self.far_b] + self.side)


class Fold:
    def __init__(self, net, at, full, full_in, vec, vec_in, out):
        self.net, self.at = net, at
        self.full, self.full_in, self.vec, self.vec_in, self.out = full, full_in, vec, vec_in, out

    def heads(self):
        at = self.at
        self.copies = []
        for k in range(1, 8):
            peer = (at.h + k) % 8
            self.copies.append(
                self.net.push(self.full.at[peer], self.full_in.at[k - 1], (peer, at.b))
            )

    def heads_sum(self):
        for copy in self.copies:
            copy.wait_recv()
        total = self.full[self.at.h].astype(F32)
        for k in range(7):
            total = total + self.full_in[k].astype(F32)
        return total

    def blocks(self):
        at = self.at
        self.copies = []
        for k in range(1, 16):
            peer = (at.b + k) % 16
            self.copies.append(
                self.net.push(self.vec.at[peer], self.vec_in.at[k - 1], (at.h, peer))
            )

    def blocks_sum(self):
        at = self.at
        for copy in self.copies:
            copy.wait_recv()
        total = self.vec[at.b].astype(F32)
        for k in range(15):
            total = total + self.vec_in[k].astype(F32)
        own = self.out.at[at.y, pl.ds(pl.multiple_of(at.c * 256 + at.b * 16, 16), 16)]
        own[...] = total.astype(BF)
        self.copies = []
        for k in range(1, 16):
            self.copies.append(self.net.push(own, own, (at.h, (at.b + k) % 16)))

    def blocks_done(self):
        for copy in self.copies:
            copy.wait_recv()

        def slot(y, c):
            return self.out.at[y, pl.ds(pl.multiple_of(c * 256, 256), 256)]

        self.gather = Gather(self.net, self.at, slot, 256)


class Scatter:
    def __init__(self, net, at, part, s, bufs):
        self.net, self.at, self.part, self.s = net, at, part, s
        self.sibr, self.ra, self.rb, self.fp, self.fm = bufs
        self.side = net.push(part.at[s, :, 1 - at.c], self.sibr.at[s], at.sib)

    def _merge(self, y):
        at, s = self.at, self.s
        self.part[s, y, at.c] = (
            self.part[s, y, at.c].astype(F32) + self.sibr[s, y].astype(F32)
        ).astype(BF)

    def merge(self):
        at, net, s = self.at, self.net, self.s
        self.side.wait_recv()
        self._merge(at.yo)
        far = self.part.at[s, at.yo, at.c]
        self.a = net.push(far.at[pl.ds(0, TOK // 2)], self.ra.at[s], at.yp)
        self.b = net.push(far.at[pl.ds(TOK // 2, TOK // 2)], self.rb.at[s], at.ym)
        self._merge(at.yu)
        self._merge(at.yd)

    def relay(self):
        at, net, s = self.at, self.net, self.s
        self.a.wait_recv()
        half = pl.ds(0, TOK // 2)
        self.part[s, at.yu, at.c, half] = (
            self.part[s, at.yu, at.c, half].astype(F32) + self.ra[s].astype(F32)
        ).astype(BF)
        self.up = net.push(self.part.at[s, at.yu, at.c], self.fp.at[s], at.yp)
        self.b.wait_recv()
        half = pl.ds(TOK // 2, TOK // 2)
        self.part[s, at.yd, at.c, half] = (
            self.part[s, at.yd, at.c, half].astype(F32) + self.rb[s].astype(F32)
        ).astype(BF)
        self.down = net.push(self.part.at[s, at.yd, at.c], self.fm.at[s], at.ym)

    def done(self):
        at, s = self.at, self.s
        self.up.wait_recv()
        self.down.wait_recv()
        self.net.settle([self.side, self.a, self.b, self.up, self.down])
        return (
            self.part[s, at.y, at.c].astype(F32) + self.sibr[s, at.y].astype(F32)
        ) + (self.fp[s].astype(F32) + self.fm[s].astype(F32))


class Weight:
    def __init__(self, net, at, ref, by_row):
        self.net, self.at, self.ref, self.by_row = net, at, ref, by_row
        self.rows, self.cols = ref.shape[1], ref.shape[2]
        self.state = [{}, {}]
        self.copies = []

    def sub(self, half, z, x, part):
        at = pl.ds(pl.multiple_of(x * 128, 128), 128)
        if self.by_row:
            width = self.cols // 2
            cols = pl.ds(half * width, width)
            if part is None:
                return self.ref.at[z, at, cols]
            return self.ref.at[z, pl.ds(pl.multiple_of(x * 128 + part * 64, 64), 64), cols]
        height = self.rows // 2
        if part is None:
            rows = pl.ds(half * height, height)
        else:
            rows = pl.ds(half * height + part * (height // 2), height // 2)
        return self.ref.at[z, rows, at]

    def block(self, half, index, part):
        if half == 0:
            if self.by_row:
                cols = pl.ds(0, self.cols // 2)
                rows = pl.ds(0, 512) if part is None else pl.ds(part * 256, 256)
                return self.ref.at[index, rows, cols]
            height = self.rows // 2
            rows = (
                pl.ds(0, height) if part is None else pl.ds(part * (height // 2), height // 2)
            )
            return self.ref.at[index, rows, pl.ds(0, 512)]
        zs = pl.ds(0, 4) if part is None else pl.ds(part * 2, 2)
        at = pl.ds(pl.multiple_of(index * 128, 128), 128)
        if self.by_row:
            return self.ref.at[zs, at, pl.ds(self.cols // 2, self.cols // 2)]
        return self.ref.at[zs, pl.ds(self.rows // 2, self.rows // 2), at]

    def _near(self, half, off, part):
        at = self.at
        if half == 0:
            return self.sub(0, at.z, (at.x + off) % 4, part)
        return self.sub(1, (at.z + off) % 4, at.x, part)

    def _far(self, half, off, part):
        at = self.at
        return self.block(half, ((at.z if half == 0 else at.x) + off) % 4, part)

    def _peers(self, half, first):
        at = self.at
        return (at.xp, at.xm) if (half == 0) == first else (at.zp, at.zm)

    def _round(self, k):
        for half in (0, 1):
            st = self.state[half]
            up, down = self._peers(half, k <= 2)
            if k == 1:
                ref = self._near(half, 0, None)
                st["u"], st["d"] = self.net.push(ref, ref, up), self.net.push(ref, ref, down)
            elif k == 2:
                st["u"].wait_recv()
                ref = self._near(half, 3, 0)
                st["fu"] = self.net.push(ref, ref, up)
                st["d"].wait_recv()
                ref = self._near(half, 1, 1)
                st["fd"] = self.net.push(ref, ref, down)
            elif k == 3:
                st["fu"].wait_recv()
                st["fd"].wait_recv()
                ref = self._far(half, 0, None)
                st["u"], st["d"] = self.net.push(ref, ref, up), self.net.push(ref, ref, down)
            elif k == 4:
                st["u"].wait_recv()
                ref = self._far(half, 3, 0)
                st["fu"] = self.net.push(ref, ref, up)
                st["d"].wait_recv()
                ref = self._far(half, 1, 1)
                st["fd"] = self.net.push(ref, ref, down)
            else:
                st["fu"].wait_recv()
                st["fd"].wait_recv()

    def step(self, k):
        first = len(self.net.copies)
        self._round(k)
        self.copies += self.net.copies[first:]

    def settle(self):
        self.net.settle(self.copies)


def rows_of(m):
    return pl.ds(pl.multiple_of(m * 256, 256), 256)


def cols_of(n):
    return pl.ds(pl.multiple_of(n * 512, 512), 512)


def heads_of(buf, s, m):
    return buf[s, pl.ds(m * 2, 2)].reshape(256, buf.shape[-1])


def rows_gather(net, at, buf, s):
    return Gather(net, at, lambda y, c: buf.at[s, y, c], TOK)


def rms(v, gain):
    return v * lax.rsqrt(jnp.mean(v * v, axis=-1, keepdims=True) + EPS) * gain


def rms_back(v, gain, grad):
    scale = lax.rsqrt(jnp.mean(v * v, axis=-1, keepdims=True) + EPS)
    scaled = gain * grad
    return scaled * scale - v * (
        jnp.mean(v * scaled, axis=-1, keepdims=True) * scale * scale * scale
    )


def put_part(part, s, m, z, value):
    part[s, pl.ds(m * 2, 2), :, :, cols_of(z)] = value.astype(BF).reshape(2, 2, TOK, 512)


def put_ext(part, s, pieces):
    part[s, :, :, :, D:] = jnp.zeros((4, 2, TOK, EXT), BF)
    for i, piece in enumerate(pieces):
        part[s, :, :, :, D + i * RANK : D + (i + 1) * RANK] = piece.astype(BF).reshape(
            4, 2, TOK, RANK
        )


def put_rows(buf, s, at, value, pieces):
    buf[s, at.y, at.c, :, :D] = value
    buf[s, at.y, at.c, :, D:] = jnp.zeros((TOK, EXT), BF)
    for i, piece in enumerate(pieces):
        buf[s, at.y, at.c, :, D + i * RANK : D + (i + 1) * RANK] = piece.astype(BF)


def grid_loop(m_count, n_count, body):
    def step(i, carry):
        body(i // n_count, i % n_count)
        return carry

    lax.fori_loop(0, m_count * n_count, step, 0)


def layer(
    index_ref, length_ref,
    tok, cot, again, fgain, inv,
    wq, wo, wg, wu, wd,
    qin, gin, uin, aout, dout, ain, din, qout, gout, uout,
    result_o, igrad_o, qi_o, qo_o, ai_o, ao_o, gi_o, go_o, ui_o, uo_o, di_o, do_o,
    w_q, w_o, w_g, w_u, w_d,
    nb, cb, part1, sib1, sib2, ra1, rb1, fp1, fm1, ra2, rb2, fp2, fm2,
    gate, up, hidden, qb, kvb, attn, lse, cosb, sinb, startb,
    midf, normed, midn, inner_a, mgrad, next_s, mid_s, cot_s, dkv, halo_in,
    a_b, d_b, q_b, g_b, u_b,
    full1, full1_in, vec1, vec1_in, full2, full2_in, vec2, vec2_in, stage8, stage2,
    send, recv, local,
):
    at = Place()
    net = Net(send, recv)
    pick = [index_ref[0, 0], index_ref[1, 0]]
    h, b = at.h, at.b

    here = pl.ds(pl.multiple_of(at.x * 128, 128), 128)
    loads = []

    def load(src, dst):
        copy = pltpu.make_async_copy(src, dst, local.at[len(loads)])
        copy.start()
        loads.append(copy)
        return copy

    load(wq, w_q.at[at.z, here, :])
    load(wo, w_o.at[at.z, :, here])
    load(wg, w_g.at[at.z, here, :])
    load(wu, w_u.at[at.z, here, :])
    load(wd, w_d.at[at.z, :, here])
    load(ain.at[:, :, pl.ds(pl.multiple_of(h * 256, 256), 256)], a_b)
    load(din.at[:, :, pl.ds(pl.multiple_of(h * 1024, 1024), 1024)], d_b)
    load(qout.at[:, :, pl.ds(pl.multiple_of(h * 512, 512), 512)], q_b)
    load(gout.at[:, :, pl.ds(pl.multiple_of(h * 1024, 1024), 1024)], g_b)
    load(uout.at[:, :, pl.ds(pl.multiple_of(h * 1024, 1024), 1024)], u_b)

    at.greet(
        [((h + k) % 8, b) for k in range(1, 8)] + [(h, (b + k) % 16) for k in range(1, 16)]
    )
    for copy in loads:
        copy.wait()
    W_Q = Weight(net, at, w_q, True)
    W_O = Weight(net, at, w_o, False)
    W_G = Weight(net, at, w_g, True)
    W_U = Weight(net, at, w_u, True)
    W_D = Weight(net, at, w_d, False)

    W_Q.step(1)
    W_O.step(1)

    g_n = []
    for s in (0, 1):
        n = rms(tok[s].astype(F32), again[...]).astype(BF)
        normed[s] = n
        put_rows(nb, s, at, n, [mm_nt(n, qin[pick[s]])])
        g_n.append(rows_gather(net, at, nb, s))
    W_Q.step(2)
    W_O.step(2)
    W_G.step(1)

    sign = jnp.where(lax.broadcasted_iota(jnp.int32, (1, 128), 1) < 64, -1.0, 1.0)

    def table(s, m):
        rows = pl.ds(pl.multiple_of(m * 64, 64), 64)
        pos = b * SPAN + m * 64 + lax.broadcasted_iota(jnp.int32, (64, 1), 0)
        start = jnp.zeros((64, 1), jnp.int32)
        end = 0
        for d in range(4):
            length = length_ref[s, d]
            end = end + length
            start = start + jnp.where(pos >= end, length, 0)
        startb[s, rows] = start
        angle = (pos - start).astype(F32) * inv[...]
        cosb[s, rows] = jnp.cos(angle)
        sinb[s, rows] = jnp.sin(angle) * sign

    grid_loop(2, 8, table)
    g_n[0].relay()
    g_n[1].relay()
    W_Q.step(3)
    W_G.step(2)

    for s in (0, 1):
        put_rows(cb, s, at, cot[s], [mm_nt(cot[s], dout[pick[s]])])
    g_n[0].last()
    g_n[1].last()
    W_Q.step(4)
    W_O.step(3)
    g_c = [rows_gather(net, at, cb, s) for s in (0, 1)]
    g_n[0].done()
    g_n[1].done()
    W_Q.step(5)
    W_G.step(3)

    halos = []
    for s in (0, 1):

        def qkv(m, unused, s=s):
            x = heads_of(nb, s, m)
            r = mm(x[:, :D], w_q[...].reshape(D, 512)) + mm(x[:, D : D + RANK], q_b[pick[s]])
            rows = rows_of(m)
            c, sn = cosb[s, rows], sinb[s, rows]

            def rot(v):
                return v * c + pltpu.roll(v, 64, 1) * sn

            for j in (0, 1):
                qb[s, j, rows] = (rot(r[:, j * 128 : (j + 1) * 128]) * SCALE).astype(BF)
            own = pl.ds(pl.multiple_of(1024 + m * 256, 256), 256)
            kvb[s, 0, own] = rot(r[:, 256:384]).astype(BF)
            kvb[s, 1, own] = r[:, 384:512].astype(BF)

        grid_loop(2, 1, qkv)
        own = kvb.at[s, :, pl.ds(1024, 512)]
        halos.append(net.push(own, kvb.at[s, :, pl.ds(512, 512)], at.next1))
        halos.append(net.push(own, kvb.at[s, :, pl.ds(0, 512)], at.next2))
    next_s[...] = nb[:, :, :, :, D:].reshape(2, SPAN, EXT)
    W_O.step(4)
    W_U.step(1)
    g_c[0].relay()
    g_c[1].relay()
    W_U.step(2)
    W_O.step(5)

    g_n[0].settle()
    g_n[1].settle()

    row = lax.broadcasted_iota(jnp.int32, (256, 1280), 0)
    col = lax.broadcasted_iota(jnp.int32, (256, 1280), 1)
    scat1 = []
    for s in (0, 1):
        halos[2 * s].wait_recv()
        halos[2 * s + 1].wait_recv()

        def attend(g, m, s=s):
            rows = rows_of(m)
            keys = pl.ds(pl.multiple_of(m * 256, 256), 1280)
            sc = mm_nt(qb[s, g, rows], kvb[s, 0, keys])
            low = startb[s, rows] - (b * SPAN - WINDOW + m * 256)
            gap = row - col + WINDOW
            ok = (gap >= 0) & (gap < WINDOW) & (col >= low)
            sc = jnp.where(ok, sc, -1e30)
            top = jnp.max(sc, axis=-1, keepdims=True)
            e = jnp.exp(sc - top)
            total = jnp.sum(e, axis=-1, keepdims=True)
            p = (e * (1.0 / total)).astype(BF)
            o = mm(p, kvb[s, 1, keys])
            attn[s, rows, pl.ds(pl.multiple_of(g * 128, 128), 128)] = o.astype(BF)
            lse[s, g, rows] = top + jnp.log(total)

        grid_loop(2, 2, attend)
        if s == 0:
            g_c[0].last()
            g_c[1].last()
            W_G.step(4)

        def out_proj(m, z, s=s):
            put_part(part1, s, m, z, mm(attn[s, rows_of(m)], w_o[z]))

        grid_loop(2, 4, out_proj)
        put_ext(part1, s, [mm_nt(attn[s], a_b[pick[s]])])
        scat1.append(Scatter(net, at, part1, s, (sib1, ra1, rb1, fp1, fm1)))
        if s == 0:
            W_U.step(3)
    g_c[0].done()
    g_c[1].done()
    scat1[0].merge()
    scat1[1].merge()
    scat1[0].relay()
    scat1[1].relay()
    W_G.step(5)
    W_D.step(1)

    g_m = []
    for s in (0, 1):
        t = scat1[s].done()
        inn = t[:, D : D + RANK]
        inner_a[s] = inn
        mid = tok[s].astype(F32) + t[:, :D] + mm(inn.astype(BF), aout[pick[s]])
        midf[s] = mid
        n = rms(mid, fgain[...]).astype(BF)
        midn[s] = n
        put_rows(nb, s, at, n, [mm_nt(n, gin[pick[s]]), mm_nt(n, uin[pick[s]])])
        g_m.append(rows_gather(net, at, nb, s))
    W_U.step(4)
    W_D.step(2)
    g_m[0].relay()
    g_m[1].relay()
    W_D.step(3)
    g_m[0].last()
    g_m[1].last()
    W_U.step(5)
    g_m[0].done()
    g_m[1].done()
    W_D.step(4)

    for s in (0, 1):

        def ffn(m, n, s=s):
            x = heads_of(nb, s, m)
            rows, cols = rows_of(m), cols_of(n)
            g = mm(x[:, :D], w_g[:, :, cols].reshape(D, 512))
            g = g + mm(x[:, D : D + RANK], g_b[pick[s], :, cols])
            u = mm(x[:, :D], w_u[:, :, cols].reshape(D, 512))
            u = u + mm(x[:, D + RANK : D + 2 * RANK], u_b[pick[s], :, cols])
            gate[s, rows, cols] = g.astype(BF)
            up[s, rows, cols] = u.astype(BF)
            hidden[s, rows, cols] = (g * jax.nn.sigmoid(g) * u).astype(BF)

        grid_loop(2, 2, ffn)
    W_D.step(5)
    mid_s[...] = nb[:, :, :, :, D:].reshape(2, SPAN, EXT)
    cot_s[...] = cb[:, :, :, :, D:].reshape(2, SPAN, EXT)
    for s in (0, 1):
        g_c[s].settle()
        g_m[s].settle()
    W_G.settle()
    W_U.settle()

    scat3 = []
    for s in (0, 1):

        def hid_back(m, n, s=s):
            x = heads_of(cb, s, m)
            rows, cols = rows_of(m), cols_of(n)
            hb = mm(x[:, D : D + RANK], d_b[pick[s], :, cols])
            for z in range(4):
                hb = hb + mm_nt(x[:, z * 512 : (z + 1) * 512], w_d[z, cols, :])
            g = gate[s, rows, cols].astype(F32)
            u = up[s, rows, cols].astype(F32)
            sg = jax.nn.sigmoid(g)
            gate[s, rows, cols] = (hb * u * sg * (1.0 + g * (1.0 - sg))).astype(BF)
            up[s, rows, cols] = (hb * g * sg).astype(BF)

        grid_loop(2, 2, hid_back)

        def mid_back(m, z, s=s):
            rows = rows_of(m)
            r = mm_nt(gate[s, rows], w_g[z]) + mm_nt(up[s, rows], w_u[z])
            put_part(part1, s, m, z, r)

        grid_loop(2, 4, mid_back)
        put_ext(part1, s, [mm_nt(gate[s], g_b[pick[s]]), mm_nt(up[s], u_b[pick[s]])])
        scat3.append(Scatter(net, at, part1, s, (sib1, ra1, rb1, fp1, fm1)))

    out1, out2 = w_g.at[:, :, pl.ds(0, 512)], w_u.at[:, :, pl.ds(0, 128)]
    fold1 = Fold(net, at, full1, full1_in, vec1, vec1_in, out1)
    fold2 = Fold(net, at, full2, full2_in, vec2, vec2_in, out2)
    scat2 = []
    for s in (0, 1):
        scat3[s].merge()

        def down(m, z, s=s):
            put_part(nb, s, m, z, mm(hidden[s, rows_of(m)], w_d[z]))

        grid_loop(2, 4, down)
        put_ext(nb, s, [mm_nt(hidden[s], d_b[pick[s]])])
        scat2.append(Scatter(net, at, nb, s, (sib2, ra2, rb2, fp2, fm2)))
    scat3[0].relay()
    scat3[1].relay()
    for s in (0, 1):
        terms = [
            mm_tn(mid_s[s], gate[s])[:RANK],
            mm_tn(mid_s[s], up[s])[RANK : 2 * RANK],
            mm_tn(cot_s[s], hidden[s])[:RANK],
        ]
        for i, term in enumerate(terms):
            for j in range(4):
                vec1[3 + 4 * i + j, :, s * 256 : (s + 1) * 256] = term[
                    :, j * 256 : (j + 1) * 256
                ].astype(BF)

    def slices(full, i, s, term):
        for j in range(8):
            full[j, i, :, s * 256 : (s + 1) * 256] = term[:, j * 256 : (j + 1) * 256].astype(BF)

    g_b2 = []
    for s in (0, 1):
        t = scat3[s].done()
        pg, pu = t[:, D : D + RANK].astype(BF), t[:, D + RANK : D + 2 * RANK].astype(BF)
        back = t[:, :D] + mm(pg, gin[pick[s]]) + mm(pu, uin[pick[s]])
        mg = cot[s].astype(F32) + rms_back(midf[s], fgain[...], back)
        mgrad[s] = mg
        bg = mg.astype(BF)
        put_rows(cb, s, at, bg, [mm_nt(bg, aout[pick[s]])])
        g_b2.append(rows_gather(net, at, cb, s))
        slices(full1, 0, s, mm_tn(pg, midn[s]))
        slices(full1, 1, s, mm_tn(pu, midn[s]))
        slices(full1, 2, s, mm_tn(inner_a[s].astype(BF), bg))
    fold1.heads()
    g_b2[0].relay()
    g_b2[1].relay()
    scat2[0].merge()
    g_b2[0].last()
    g_b2[1].last()
    scat2[1].merge()
    vec1[0:3] = fold1.heads_sum().astype(BF)
    g_b2[0].done()
    g_b2[1].done()

    def attn_back(s):
        def step(m, unused):
            x = heads_of(cb, s, m)
            r = mm(x[:, D : D + RANK], a_b[pick[s]])
            for z in range(4):
                r = r + mm_nt(x[:, z * 512 : (z + 1) * 512], w_o[z])
            hidden[s, rows_of(m), 512:768] = r.astype(BF)

        grid_loop(2, 1, step)
        e = cb[s, :, :, :, D:].reshape(SPAN, EXT)
        vec1[15, :, s * 256 : (s + 1) * 256] = mm_tn(e, attn[s])[:RANK].astype(BF)

    attn_back(0)
    attn_back(1)
    fold1.blocks()
    back_halos = []
    for s in (0, 1):
        dkv[...] = jnp.zeros(dkv.shape, F32)

        def attend_back(g, m, s=s):
            rows = rows_of(m)
            keys = pl.ds(pl.multiple_of(m * 256, 256), 1280)
            mine = pl.ds(pl.multiple_of(g * 128, 128), 128)
            q, k = qb[s, g, rows], kvb[s, 0, keys]
            do = hidden[s, rows, pl.ds(pl.multiple_of(512 + g * 128, 128), 128)]
            low = startb[s, rows] - (b * SPAN - WINDOW + m * 256)
            gap = row - col + WINDOW
            ok = (gap >= 0) & (gap < WINDOW) & (col >= low)
            p = jnp.where(ok, jnp.exp(mm_nt(q, k) - lse[s, g, rows]), 0.0)
            vg = mm_nt(do, kvb[s, 1, keys])
            delta = jnp.sum(p * vg, axis=-1, keepdims=True)
            sg = (p * (vg - delta)).astype(BF)
            dq = mm(sg, k) * SCALE
            hidden[s, rows, mine] = (
                dq * cosb[s, rows] - pltpu.roll(dq, 64, 1) * sinb[s, rows]
            ).astype(BF)
            dkv[0, keys] += mm_tn(sg, q)
            dkv[1, keys] += mm_tn(p.astype(BF), do)

        grid_loop(2, 2, attend_back)
        for hop in (0, 1, 2):
            for i in (0, 1):
                at_col = hop * 256 + i * 128
                gate[s, :, at_col : at_col + 128] = dkv[
                    i, (2 - hop) * SPAN : (3 - hop) * SPAN
                ].astype(BF)
            if hop == 0:
                continue
            back_halos.append(
                net.push(
                    gate.at[s, :, pl.ds(hop * 256, 256)],
                    halo_in.at[s, hop - 1],
                    at.prev1 if hop == 1 else at.prev2,
                )
            )
        if s == 0:
            scat2[0].relay()
            scat2[1].relay()
            fold1.blocks_sum()
    for s in (0, 1):
        t = scat2[s].done()
        inn = t[:, D : D + RANK].astype(BF)
        midf[s] = midf[s] + t[:, :D] + mm(inn, dout[pick[s]])
        slices(full2, 1, s, mm_tn(inn, cot[s]))
    fold1.blocks_done()

    scat4 = []
    for s in (0, 1):
        back_halos[2 * s].wait_recv()
        back_halos[2 * s + 1].wait_recv()

        def key_back(m, unused, s=s):
            rows = rows_of(m)
            dk, dv = [
                gate[s, rows, i * 128 : (i + 1) * 128].astype(F32)
                + halo_in[s, 0, rows, i * 128 : (i + 1) * 128].astype(F32)
                + halo_in[s, 1, rows, i * 128 : (i + 1) * 128].astype(F32)
                for i in (0, 1)
            ]
            hidden[s, rows, 256:384] = (
                dk * cosb[s, rows] - pltpu.roll(dk, 64, 1) * sinb[s, rows]
            ).astype(BF)
            hidden[s, rows, 384:512] = dv.astype(BF)

        grid_loop(2, 1, key_back)

        def qkv_back(m, z, s=s):
            put_part(part1, s, m, z, mm_nt(hidden[s, rows_of(m), :512], w_q[z]))

        grid_loop(2, 4, qkv_back)
        raw = hidden[s, :, :512]
        put_ext(part1, s, [mm_nt(raw, q_b[pick[s]])])
        scat4.append(Scatter(net, at, part1, s, (sib1, ra1, rb1, fp1, fm1)))
        term = mm_tn(next_s[s], raw)[:RANK]
        for j in range(4):
            vec2[s * 8 + 4 + j] = term[:, j * 128 : (j + 1) * 128].astype(BF)
        if s == 1:
            fold1.gather.relay()
        scat4[s].merge()
    scat4[0].relay()
    scat4[1].relay()
    fold1.gather.last()
    for s in (0, 1):
        t = scat4[s].done()
        p = t[:, D : D + RANK].astype(BF)
        back = t[:, :D] + mm(p, qin[pick[s]])
        mgrad[s] = mgrad[s] + rms_back(tok[s].astype(F32), again[...], back)
        slices(full2, 0, s, mm_tn(p, normed[s]))
    fold2.heads()
    writes = [
        pltpu.make_async_copy(midf, result_o, local.at[0]),
        pltpu.make_async_copy(mgrad, igrad_o, local.at[1]),
    ]
    for copy in writes:
        copy.start()

    swap = pick[0] == 1

    def found(buf, j, i, width):
        row0 = (j % 2) * 256 + i * RANK
        return buf[j // 2, row0 : row0 + RANK, :width]

    def emit(stage, out, sem, parts):
        for cols, (first, second) in parts:
            first, second = first.astype(F32), second.astype(F32)
            stage[0, :, cols] = jnp.where(swap, second, first)
            stage[1, :, cols] = jnp.where(swap, first, second)
        copy = pltpu.make_async_copy(stage, out, local.at[sem])
        copy.start()
        return copy

    fold1.gather.done()
    wide = [go_o, uo_o, di_o]
    for i in range(3):
        parts = []
        for j in range(8):
            for k in range(4):
                block = found(w_g, j, 3 + 4 * i + k, 512)
                parts.append((pl.ds(j * 1024 + k * 256, 256), (block[:, :256], block[:, 256:])))
        copy = emit(stage8, wide[i], 2, parts)
        copy.wait()
    small = []
    for i, (index, out) in enumerate([(0, gi_o), (1, ui_o), (2, ao_o), (15, ai_o)]):
        parts = []
        for j in range(8):
            block = found(w_g, j, index, 512)
            parts.append((pl.ds(j * 256, 256), (block[:, :256], block[:, 256:])))
        small.append(emit(stage2.at[i], out, 3 + i, parts))

    total = fold2.heads_sum()
    for i in (0, 1):
        for s in (0, 1):
            for j in (0, 1):
                vec2[s * 8 + 2 * i + j] = total[i, :, s * 256 + j * 128 : s * 256 + (j + 1) * 128].astype(BF)
    fold2.blocks()
    fold2.blocks_sum()
    fold2.blocks_done()
    fold2.gather.relay()
    fold2.gather.last()
    fold2.gather.done()
    for i, out in enumerate([qi_o, do_o]):
        parts = []
        for j in range(8):
            for k in range(2):
                first = found(w_u, j, 2 * i + k, 128)
                second = found(w_u, j, 8 + 2 * i + k, 128)
                parts.append((pl.ds(j * 256 + k * 128, 128), (first, second)))
        small[i].wait()
        small[i] = emit(stage2.at[i], out, 3 + i, parts)
    parts = []
    for j in range(8):
        for k in range(4):
            first = found(w_u, j, 4 + k, 128)
            second = found(w_u, j, 12 + k, 128)
            parts.append((pl.ds(j * 512 + k * 128, 128), (first, second)))
    writes.append(emit(stage8.at[:, :, pl.ds(0, 4096)], qo_o, 2, parts))
    net.drain()
    for copy in writes + small:
        copy.wait()


def call_layer(args):
    vm = lambda *shape, t=BF: pltpu.VMEM(shape, t)
    rs = lambda: [vm(2, TOK // 2, CW), vm(2, TOK // 2, CW), vm(2, TOK, CW), vm(2, TOK, CW)]
    narrow, wide = ((2, RANK, D), F32), ((2, RANK, 8192), F32)
    outs = [
        ((2, TOK, D), F32), ((2, TOK, D), F32), narrow, ((2, RANK, 4096), F32), narrow, narrow,
        narrow, wide, narrow, wide, wide, narrow,
    ]
    scratch = (
        [vm(4, 512, 512), vm(4, 256, 512), vm(4, 512, 1024), vm(4, 512, 1024), vm(4, 1024, 512)]
        + [vm(2, 4, 2, TOK, CW)] * 3
        + [vm(2, 4, TOK, CW), vm(2, 4, TOK, CW)]
        + rs() + rs()
        + [vm(2, SPAN, 1024)] * 3
        + [vm(2, 2, SPAN, 128), vm(2, 2, 1536, 128), vm(2, SPAN, 256), vm(2, 2, SPAN, 1, t=F32)]
        + [vm(2, SPAN, 128, t=F32)] * 2
        + [vm(2, SPAN, 1, t=jnp.int32)]
        + [vm(2, TOK, D, t=F32), vm(2, TOK, D), vm(2, TOK, D), vm(2, TOK, RANK, t=F32)]
        + [vm(2, TOK, D, t=F32)] + [vm(2, SPAN, EXT)] * 3
        + [vm(2, 1536, 128, t=F32), vm(2, 2, SPAN, 256)]
        + [vm(2, RANK, 256), vm(2, RANK, 1024), vm(2, RANK, 512), vm(2, RANK, 1024), vm(2, RANK, 1024)]
        + [vm(8, 3, RANK, 512), vm(7, 3, RANK, 512), vm(16, RANK, 512), vm(15, RANK, 512)]
        + [vm(8, 2, RANK, 512), vm(7, 2, RANK, 512), vm(16, RANK, 128), vm(15, RANK, 128)]
        + [vm(2, RANK, 8192, t=F32), vm(4, 2, RANK, D, t=F32)]
        + [pltpu.SemaphoreType.DMA((320,)), pltpu.SemaphoreType.DMA((320,)), pltpu.SemaphoreType.DMA((10,))]
    )
    smem = pl.BlockSpec(memory_space=pltpu.SMEM)
    vmem = pl.BlockSpec(memory_space=pltpu.VMEM)
    hbm = pl.BlockSpec(memory_space=pl.ANY)
    return pl.pallas_call(
        layer,
        out_shape=[jax.ShapeDtypeStruct(shape, kind) for shape, kind in outs],
        in_specs=[smem] * 2 + [vmem] * 5 + [hbm] * 5 + [vmem] * 5 + [hbm] * 5,
        out_specs=[hbm] * len(outs),
        scratch_shapes=scratch,
        compiler_params=pltpu.CompilerParams(
            collective_id=0, has_side_effects=True, vmem_limit_bytes=VMEM_BYTES
        ),
    )(*args)


def body(
    tokens, cotangent, doc_lengths, adapter_index, attn_gain, ffn_gain,
    w_qkv, w_out, w_gate, w_up, w_down,
    qkv_in, qkv_out, attn_in, attn_out, gate_in, gate_out, up_in, up_out, down_in, down_out,
):
    flip = lambda g: jnp.swapaxes(g, 1, 2)
    half = jnp.arange(64, dtype=F32)
    inverse = THETA ** (-(half * 2.0 / 128))
    inv = jnp.concatenate([inverse, inverse])[None]
    result, igrad, qi, qo, ai, ao, gi, go, ui, uo, di, do = call_layer((
        adapter_index, doc_lengths, tokens, cotangent, attn_gain[None], ffn_gain[None], inv,
        w_qkv, w_out, w_gate, w_up, w_down,
        flip(qkv_in), flip(gate_in), flip(up_in), attn_out, down_out, flip(attn_in), flip(down_in),
        qkv_out, gate_out, up_out,
    ))
    return (
        result, igrad, flip(qi), qo, flip(ai), ao, flip(gi), go, flip(ui), uo, flip(di), do
    )


def solution(mesh):
    row = P(None, ("blk", "head"), None)
    return jax.shard_map(
        body,
        mesh=mesh,
        in_specs=(row, row) + (P(),) * 4
        + (P("blk", "head"), P("head", "blk"), P("blk", "head"), P("blk", "head"), P("head", "blk"))
        + (P(),) * 10,
        out_specs=(row, row) + (P(),) * 10,
        check_vma=False,
    )
```

profile of v0, /device:TPU:1, one launch (start us, length us, event | category | flops | bytes accessed | tf_op | source)
XLA Modules:
  0.0 320.0 jit_solution(18238220303776377838)
XLA Ops:
  0.7 0.0 copy-start.11
  0.7 0.6 maximum_bitcast_fusion.inv
  1.3 0.1 copy-done.11
  1.3 0.6 copy.33.index_ref
  2.0 305.0 %shard_map.292 = (f32[2,64,2048]{2,1,0:T(8,128)}, f32[2,64,2048]{2,1,0:T(8,128)}, f32[2,16,2048]{2,1,0:T(8,128)}, f32[2,16,4096]{2,1,0:T(8,128)}, f32[2,16,2048]...) custom-call(s32[2,1]{1,0:T(2,128)} %copy.33.index_ref, ...), custom_call_target="tpu_custom_call" | custom-call | tf_op jit(solution)/shard_map/pallas_call | solution.py:892
  307.0 0.0 copy-start.3
  307.0 2.4 copy.46
  309.4 1.0 copy.47
  310.3 0.1 copy-done.10
  310.5 0.7 copy.48
  311.2 0.4 copy-done.4
  311.6 0.8 copy.49
  312.4 0.3 copy-done.9
  312.7 0.7 copy.50
  313.4 0.7 copy.51
  314.1 0.7 copy.52
  314.8 1.0 copy.53
  315.8 0.1 copy-done.6
  315.9 0.7 copy.54
  316.6 1.0 copy.55
  317.6 0.6 copy-done
  318.2 1.0 copy.56
  319.2 0.1 copy-done.5
  319.3 0.7 copy.57
  (16 shorter events, 0.0 us)
Async XLA Ops:
  0.7 0.7 copy-start.11
  307.0 2.4 copy-start.3
  309.4 1.1 copy-start.10
  310.5 1.1 copy-start.4
  311.6 1.1 copy-start.9
  311.6 1.8 copy-start.8
  311.6 2.5 copy-start.7
  312.7 2.1 copy-start.2
  314.8 1.1 copy-start.6
  314.8 1.8 copy-start.1
  316.6 1.6 copy-start
  318.2 1.1 copy-start.5
where the time goes:
time: 320 us
  Pallas kernels  305 us (95%)
  local copies, waits for them, and re-layouts  13.7 us (4%)
    pallas_call x1, Pallas kernels, call_layer(): pl.pallas_call(layer, out_shape=[jax.ShapeDtypeStruct(shape, kind) for sh...  305 us
    unnamed x37, local copies, waits for them, and re-layouts  13.7 us

commit v1 on v0

v1 whole, which is shorter than its diff:
```python
from functools import partial

import jax
import jax.numpy as jnp
import numpy as np
from jax import lax
from jax.experimental import pallas as pl
from jax.experimental.pallas import tpu as pltpu
from jax.sharding import PartitionSpec as P

MESH = pl.DeviceIdType.MESH
BF = jnp.bfloat16
F32 = jnp.float32
D = 2048
EXT = 128
CW = D + EXT
RANK = 16
WINDOW = 1024
EPS = 1e-05
THETA = 1000000.0
Y, CORES, Z, X = 4, 2, 4, 4
TOK = 64
SPAN = 512
SCALE = 128 ** (-0.5)
VMEM_BYTES = 66977792
N_SEMS = 180


def mm(a, b):
    return jnp.dot(a, b, preferred_element_type=F32)


def mm_nt(a, b):
    return lax.dot_general(a, b, (((1,), (1,)), ((), ())), preferred_element_type=F32)


def mm_tn(a, b):
    return lax.dot_general(a, b, (((0,), (0,)), ((), ())), preferred_element_type=F32)


class Place:
    def __init__(self):
        h = lax.axis_index("head")
        b = lax.axis_index("blk")
        self.h, self.b = h, b
        self.y, self.c = h // 2, h % 2
        self.z, self.x = b // 4, b % 4
        y, c, z, x = self.y, self.c, self.z, self.x
        self.yu, self.yd, self.yo = (y + 1) % 4, (y + 3) % 4, (y + 2) % 4
        self.xu, self.xd = (x + 1) % 4, (x + 3) % 4
        self.zu, self.zd = (z + 1) % 4, (z + 3) % 4
        self.sib = (y * 2 + (1 - c), b)
        self.yp, self.ym = (self.yu * 2 + c, b), (self.yd * 2 + c, b)
        self.xp, self.xm = (h, z * 4 + self.xu), (h, z * 4 + self.xd)
        self.zp, self.zm = (h, self.zu * 4 + x), (h, self.zd * 4 + x)
        self.next1, self.next2 = (h, (b + 1) % 16), (h, (b + 2) % 16)
        self.prev1, self.prev2 = (h, (b + 15) % 16), (h, (b + 14) % 16)

    def greet(self, peers):
        barrier = pltpu.get_barrier_semaphore()
        for peer in peers:
            pl.semaphore_signal(barrier, inc=1, device_id=peer, device_id_type=MESH)
        pl.semaphore_wait(barrier, len(peers))


class Net:
    def __init__(self, send, recv):
        self.send, self.recv, self.count, self.copies = send, recv, 0, []

    def ids(self, n):
        first = self.count
        self.count += n
        return list(range(first, first + n))

    def make(self, src, dst, peer, i):
        return pltpu.make_async_remote_copy(
            src_ref=src,
            dst_ref=dst,
            send_sem=self.send.at[i],
            recv_sem=self.recv.at[i],
            device_id=peer,
            device_id_type=MESH,
        )

    def push(self, src, dst, peer, i):
        copy = self.make(src, dst, peer, i)
        copy.start()
        self.copies.append(copy)
        return copy

    def spread(self, pairs, whole, i):
        for src, dst, peer in pairs:
            self.make(src, dst, peer, i).start()
        copy = self.make(whole, whole, pairs[0][2], i)
        self.copies.append(copy)
        return copy

    def settle(self, copies):
        for copy in copies:
            copy.wait_send()
            self.copies = [other for other in self.copies if other is not copy]

    def drain(self):
        self.settle(list(self.copies))


class Gather:
    def __init__(self, net, at, slot, extent, ids):
        self.net, self.at, self.slot, self.half, self.ids = net, at, slot, extent // 2, ids
        own = slot(at.y, at.c)
        self.up = net.push(own, own, at.yp, ids[0])
        self.down = net.push(own, own, at.ym, ids[1])
        self.side = [net.push(own, own, at.sib, ids[2])]

    def relay(self):
        at, net, half, ids = self.at, self.net, self.half, self.ids
        below = self.slot(at.yd, at.c)
        above = self.slot(at.yu, at.c)
        self.up.wait_recv()
        part = below.at[pl.ds(0, half)]
        self.far_a = net.push(part, part, at.yp, ids[3])
        self.side.append(net.push(below, below, at.sib, ids[4]))
        self.down.wait_recv()
        part = above.at[pl.ds(half, half)]
        self.far_b = net.push(part, part, at.ym, ids[5])
        self.side.append(net.push(above, above, at.sib, ids[6]))

    def last(self):
        at, net, half, ids = self.at, self.net, self.half, self.ids
        far = self.slot(at.yo, at.c)
        self.far_a.wait_recv()
        part = far.at[pl.ds(0, half)]
        self.side.append(net.push(part, part, at.sib, ids[7]))
        self.far_b.wait_recv()
        part = far.at[pl.ds(half, half)]
        self.side.append(net.push(part, part, at.sib, ids[8]))

    def done(self):
        for copy in self.side:
            copy.wait_recv()

    def settle(self):
        self.net.settle([self.up, self.down, self.far_a, self.far_b] + self.side)


class Fold:
    def __init__(self, net, at, full, full_in, vec, vec_in, out, near):
        self.net, self.at = net, at
        self.full, self.full_in, self.vec, self.vec_in, self.out = full, full_in, vec, vec_in, out
        self.ids, self.near = net.ids(2), near

    def heads(self):
        at = self.at
        pairs = []
        for k in range(1, 8):
            peer = (at.h + k) % 8
            pairs.append((self.full.at[peer], self.full_in.at[k - 1], (peer, at.b)))
        self.copy = self.net.spread(pairs, self.full_in, self.ids[0])

    def heads_sum(self):
        self.copy.wait_recv()
        total = self.full[self.at.h].astype(F32)
        for k in range(7):
            total = total + self.full_in[k].astype(F32)
        return total

    def blocks(self):
        at = self.at
        pairs = []
        for k in range(1, 16):
            peer = (at.b + k) % 16
            pairs.append((self.vec.at[peer], self.vec_in.at[k - 1], (at.h, peer)))
        self.copy = self.net.spread(pairs, self.vec_in, self.ids[1])

    def blocks_sum(self):
        at = self.at
        self.copy.wait_recv()
        total = self.vec[at.b].astype(F32)
        for k in range(15):
            total = total + self.vec_in[k].astype(F32)
        own = self.out.at[at.z, pl.ds(pl.multiple_of(at.x * 128 + at.h * 16, 16), 16)]
        own[...] = total.astype(BF)
        self.copies = [
            self.net.push(own, own, ((at.h + k) % 8, at.b), self.near[k - 1]) for k in range(1, 8)
        ]

    def near_done(self):
        for copy in self.copies:
            copy.wait_recv()
        self.net.settle(self.copies)

    def far(self, ids):
        at = self.at
        own = self.out.at[at.z, pl.ds(pl.multiple_of(at.x * 128, 128), 128)]
        self.copies = [
            self.net.push(own, own, (at.h, (at.b + k) % 16), ids[k - 1]) for k in range(1, 16)
        ]

    def far_done(self):
        for copy in self.copies:
            copy.wait_recv()


class Scatter:
    def __init__(self, net, at, part, s, bufs, ids):
        self.net, self.at, self.part, self.s, self.ids = net, at, part, s, ids
        self.sibr, self.ra, self.rb, self.fp, self.fm = bufs
        self.side = net.push(part.at[s, :, 1 - at.c], self.sibr.at[s], at.sib, ids[0])

    def _merge(self, y):
        at, s = self.at, self.s
        self.part[s, y, at.c] = (
            self.part[s, y, at.c].astype(F32) + self.sibr[s, y].astype(F32)
        ).astype(BF)

    def merge(self):
        at, net, s = self.at, self.net, self.s
        self.side.wait_recv()
        self._merge(at.yo)
        far = self.part.at[s, at.yo, at.c]
        self.a = net.push(far.at[pl.ds(0, TOK // 2)], self.ra.at[s], at.yp, self.ids[1])
        self.b = net.push(far.at[pl.ds(TOK // 2, TOK // 2)], self.rb.at[s], at.ym, self.ids[2])
        self._merge(at.yu)
        self._merge(at.yd)

    def relay(self):
        at, net, s = self.at, self.net, self.s
        self.a.wait_recv()
        half = pl.ds(0, TOK // 2)
        self.part[s, at.yu, at.c, half] = (
            self.part[s, at.yu, at.c, half].astype(F32) + self.ra[s].astype(F32)
        ).astype(BF)
        self.up = net.push(self.part.at[s, at.yu, at.c], self.fp.at[s], at.yp, self.ids[3])
        self.b.wait_recv()
        half = pl.ds(TOK // 2, TOK // 2)
        self.part[s, at.yd, at.c, half] = (
            self.part[s, at.yd, at.c, half].astype(F32) + self.rb[s].astype(F32)
        ).astype(BF)
        self.down = net.push(self.part.at[s, at.yd, at.c], self.fm.at[s], at.ym, self.ids[4])

    def done(self):
        at, s = self.at, self.s
        self.up.wait_recv()
        self.down.wait_recv()
        self.net.settle([self.side, self.a, self.b, self.up, self.down])
        return (
            self.part[s, at.y, at.c].astype(F32) + self.sibr[s, at.y].astype(F32)
        ) + (self.fp[s].astype(F32) + self.fm[s].astype(F32))


class Weight:
    def __init__(self, net, at, ref, by_row, ids):
        self.net, self.at, self.ref, self.by_row, self.ids = net, at, ref, by_row, ids
        self.rows, self.cols = ref.shape[1], ref.shape[2]
        self.state = [{}, {}]
        self.copies = []

    def sub(self, half, z, x, part):
        at = pl.ds(pl.multiple_of(x * 128, 128), 128)
        if self.by_row:
            width = self.cols // 2
            cols = pl.ds(half * width, width)
            if part is None:
                return self.ref.at[z, at, cols]
            return self.ref.at[z, pl.ds(pl.multiple_of(x * 128 + part * 64, 64), 64), cols]
        height = self.rows // 2
        if part is None:
            rows = pl.ds(half * height, height)
        else:
            rows = pl.ds(half * height + part * (height // 2), height // 2)
        return self.ref.at[z, rows, at]

    def block(self, half, index, part):
        if half == 0:
            if self.by_row:
                cols = pl.ds(0, self.cols // 2)
                rows = pl.ds(0, 512) if part is None else pl.ds(part * 256, 256)
                return self.ref.at[index, rows, cols]
            height = self.rows // 2
            rows = (
                pl.ds(0, height) if part is None else pl.ds(part * (height // 2), height // 2)
            )
            return self.ref.at[index, rows, pl.ds(0, 512)]
        zs = pl.ds(0, 4) if part is None else pl.ds(part * 2, 2)
        at = pl.ds(pl.multiple_of(index * 128, 128), 128)
        if self.by_row:
            return self.ref.at[zs, at, pl.ds(self.cols // 2, self.cols // 2)]
        return self.ref.at[zs, pl.ds(self.rows // 2, self.rows // 2), at]

    def _near(self, half, off, part):
        at = self.at
        if half == 0:
            return self.sub(0, at.z, (at.x + off) % 4, part)
        return self.sub(1, (at.z + off) % 4, at.x, part)

    def _far(self, half, off, part):
        at = self.at
        return self.block(half, ((at.z if half == 0 else at.x) + off) % 4, part)

    def _peers(self, half, first):
        at = self.at
        return (at.xp, at.xm) if (half == 0) == first else (at.zp, at.zm)

    def _push(self, ref, peer, half, k, way):
        return self.net.push(ref, ref, peer, self.ids[half * 8 + (k - 1) * 2 + way])

    def _round(self, k):
        for half in (0, 1):
            st = self.state[half]
            near = self._near if k <= 2 else self._far
            up, down = self._peers(half, k <= 2)
            if k > 1:
                st[0].wait_recv()
                st[1].wait_recv()
            if k in (1, 3):
                ref = near(half, 0, None)
                st[0] = self._push(ref, up, half, k, 0)
                st[1] = self._push(ref, down, half, k, 1)
            elif k in (2, 4):
                st[0] = self._push(near(half, 3, 0), up, half, k, 0)
                st[1] = self._push(near(half, 1, 1), down, half, k, 1)

    def step(self, k):
        first = len(self.net.copies)
        self._round(k)
        self.copies += self.net.copies[first:]

    def settle(self):
        self.net.settle(self.copies)


def rows_of(m):
    return pl.ds(pl.multiple_of(m * 256, 256), 256)


def cols_of(n):
    return pl.ds(pl.multiple_of(n * 512, 512), 512)


def heads_of(buf, s, m):
    return buf[s, pl.ds(m * 2, 2)].reshape(256, buf.shape[-1])


def rows_gather(net, at, buf, s, ids):
    return Gather(net, at, lambda y, c: buf.at[s, y, c], TOK, ids)


def rms(v, gain):
    return v * lax.rsqrt(jnp.mean(v * v, axis=-1, keepdims=True) + EPS) * gain


def rms_back(v, gain, grad):
    scale = lax.rsqrt(jnp.mean(v * v, axis=-1, keepdims=True) + EPS)
    scaled = gain * grad
    return scaled * scale - v * (
        jnp.mean(v * scaled, axis=-1, keepdims=True) * scale * scale * scale
    )


def put_part(part, s, m, z, value):
    part[s, pl.ds(m * 2, 2), :, :, cols_of(z)] = value.astype(BF).reshape(2, 2, TOK, 512)


def put_ext(part, s, pieces):
    part[s, :, :, :, D:] = jnp.zeros((4, 2, TOK, EXT), BF)
    for i, piece in enumerate(pieces):
        part[s, :, :, :, D + i * RANK : D + (i + 1) * RANK] = piece.astype(BF).reshape(
            4, 2, TOK, RANK
        )


def put_rows(buf, s, at, value, pieces):
    buf[s, at.y, at.c, :, :D] = value
    buf[s, at.y, at.c, :, D:] = jnp.zeros((TOK, EXT), BF)
    for i, piece in enumerate(pieces):
        buf[s, at.y, at.c, :, D + i * RANK : D + (i + 1) * RANK] = piece.astype(BF)


def grid_loop(m_count, n_count, body):
    def step(i, carry):
        body(i // n_count, i % n_count)
        return carry

    lax.fori_loop(0, m_count * n_count, step, 0)


def layer(
    index_ref, length_ref,
    tok, cot, again, fgain, inv,
    wq, wo, wg, wu, wd,
    qin, gin, uin, aout, dout, ain, din, qout, gout, uout,
    result_o, igrad_o, sums1_o, sums2_o,
    w_q, w_o, w_g, w_u, w_d,
    nb, cb, part1, sib1, sib2, ra1, rb1, fp1, fm1, ra2, rb2, fp2, fm2,
    gate, up, hidden, qb, kvb, attn, lse, cosb, sinb, startb,
    midf, normed, midn, inner_a, mgrad, next_s, mid_s, cot_s, dkv, halo_in,
    a_b, d_b, q_b, g_b, u_b,
    full1, full1_in, vec1, vec1_in, full2, full2_in, vec2, vec2_in, px, px_in,
    send, recv, local,
):
    at = Place()
    net = Net(send, recv)
    pick = [index_ref[0], index_ref[1]]
    h, b = at.h, at.b
    both = (0, 1)

    here = pl.ds(pl.multiple_of(at.x * 128, 128), 128)
    loads = []

    def load(src, dst):
        copy = pltpu.make_async_copy(src, dst, local.at[len(loads)])
        copy.start()
        loads.append(copy)

    load(wq, w_q.at[at.z, here, :])
    load(wo, w_o.at[at.z, :, here])
    load(wg, w_g.at[at.z, here, :])
    load(wu, w_u.at[at.z, here, :])
    load(wd, w_d.at[at.z, :, here])
    load(qout.at[:, :, pl.ds(pl.multiple_of(h * 512, 512), 512)], q_b)
    load(ain.at[:, :, pl.ds(pl.multiple_of(h * 256, 256), 256)], a_b)
    load(din.at[:, :, pl.ds(pl.multiple_of(h * 1024, 1024), 1024)], d_b)
    load(gout.at[:, :, pl.ds(pl.multiple_of(h * 1024, 1024), 1024)], g_b)
    load(uout.at[:, :, pl.ds(pl.multiple_of(h * 1024, 1024), 1024)], u_b)
    at.greet(
        [((h + k) % 8, b) for k in range(1, 8)] + [(h, (b + k) % 16) for k in range(1, 16)]
    )

    q_ids = net.ids(16)
    W_Q = Weight(net, at, w_q, True, q_ids)
    W_O = Weight(net, at, w_o, False, net.ids(16))
    W_G = Weight(net, at, w_g, True, net.ids(16))
    W_U = Weight(net, at, w_u, True, net.ids(16))
    W_D = Weight(net, at, w_d, False, net.ids(16))
    n_ids = [net.ids(9), net.ids(9)]
    c_ids = [net.ids(9), net.ids(9)]
    s_ids = [net.ids(5), net.ids(5)]
    t_ids = [net.ids(5), net.ids(5)]
    near_ids = net.ids(7)
    halo_ids = net.ids(8)
    px_ids = net.ids(2)
    out1, out2 = w_g.at[:, :, pl.ds(0, 512)], w_u.at[:, :, pl.ds(0, 128)]
    fold1 = Fold(net, at, full1, full1_in, vec1, vec1_in, out1, near_ids)
    fold2 = Fold(net, at, full2, full2_in, vec2, vec2_in, out2, near_ids)
    set1, set2 = (sib1, ra1, rb1, fp1, fm1), (sib2, ra2, rb2, fp2, fm2)

    def norm_in(s):
        n = rms(tok[s].astype(F32), again[...]).astype(BF)
        normed[s] = n
        put_rows(nb, s, at, n, [mm_nt(n, qin[pick[s]])])

    sign = jnp.where(lax.broadcasted_iota(jnp.int32, (1, 128), 1) < 64, -1.0, 1.0)

    def table(s, m):
        rows = pl.ds(pl.multiple_of(m * 64, 64), 64)
        pos = b * SPAN + m * 64 + lax.broadcasted_iota(jnp.int32, (64, 1), 0)
        start = jnp.zeros((64, 1), jnp.int32)
        end = 0
        for d in range(4):
            length = length_ref[s, d]
            end = end + length
            start = start + jnp.where(pos >= end, length, 0)
        startb[s, rows] = start
        angle = (pos - start).astype(F32) * inv[...]
        cosb[s, rows] = jnp.cos(angle)
        sinb[s, rows] = jnp.sin(angle) * sign

    def cot_in(s):
        put_rows(cb, s, at, cot[s], [mm_nt(cot[s], dout[pick[s]])])

    def qkv(s):
        def step(m, unused):
            x = heads_of(nb, s, m)
            r = mm(x[:, :D], w_q[...].reshape(D, 512)) + mm(x[:, D : D + RANK], q_b[pick[s]])
            rows = rows_of(m)
            c, sn = cosb[s, rows], sinb[s, rows]

            def rot(v):
                return v * c + pltpu.roll(v, 64, 1) * sn

            for j in both:
                qb[s, j, rows] = (rot(r[:, j * 128 : (j + 1) * 128]) * SCALE).astype(BF)
            own = pl.ds(pl.multiple_of(1024 + m * 256, 256), 256)
            kvb[s, 0, own] = rot(r[:, 256:384]).astype(BF)
            kvb[s, 1, own] = r[:, 384:512].astype(BF)

        grid_loop(2, 1, step)
        next_s[s] = nb[s, :, :, :, D:].reshape(SPAN, EXT)

    def halo(s):
        own = kvb.at[s, :, pl.ds(1024, 512)]
        return [
            net.push(own, kvb.at[s, :, pl.ds(512, 512)], at.next1, halo_ids[2 * s]),
            net.push(own, kvb.at[s, :, pl.ds(0, 512)], at.next2, halo_ids[2 * s + 1]),
        ]

    row = lax.broadcasted_iota(jnp.int32, (256, 1280), 0)
    col = lax.broadcasted_iota(jnp.int32, (256, 1280), 1)

    def allowed(s, m):
        low = startb[s, rows_of(m)] - (b * SPAN - WINDOW + m * 256)
        gap = row - col + WINDOW
        return (gap >= 0) & (gap < WINDOW) & (col >= low)

    def keys_of(m):
        return pl.ds(pl.multiple_of(m * 256, 256), 1280)

    def attend(s, g):
        def step(m, unused):
            rows, keys = rows_of(m), keys_of(m)
            sc = mm_nt(qb[s, g, rows], kvb[s, 0, keys])
            sc = jnp.where(allowed(s, m), sc, -1e30)
            top = jnp.max(sc, axis=-1, keepdims=True)
            e = jnp.exp(sc - top)
            total = jnp.sum(e, axis=-1, keepdims=True)
            p = (e * (1.0 / total)).astype(BF)
            o = mm(p, kvb[s, 1, keys])
            attn[s, rows, g * 128 : (g + 1) * 128] = o.astype(BF)
            lse[s, g, rows] = top + jnp.log(total)

        grid_loop(2, 1, step)

    def out_proj(s):
        grid_loop(
            2, 4, lambda m, z: put_part(part1, s, m, z, mm(attn[s, rows_of(m)], w_o[z]))
        )
        put_ext(part1, s, [mm_nt(attn[s], a_b[pick[s]])])
        return Scatter(net, at, part1, s, set1, s_ids[s])

    def middle(s, t):
        inn = t[:, D : D + RANK]
        inner_a[s] = inn
        mid = tok[s].astype(F32) + t[:, :D] + mm(inn.astype(BF), aout[pick[s]])
        midf[s] = mid
        n = rms(mid, fgain[...]).astype(BF)
        midn[s] = n
        put_rows(nb, s, at, n, [mm_nt(n, gin[pick[s]]), mm_nt(n, uin[pick[s]])])
        return rows_gather(net, at, nb, s, n_ids[s])

    def ffn(s):
        def step(m, n):
            x = heads_of(nb, s, m)
            rows, cols = rows_of(m), cols_of(n)
            g = mm(x[:, :D], w_g[:, :, cols].reshape(D, 512))
            g = g + mm(x[:, D : D + RANK], g_b[pick[s], :, cols])
            u = mm(x[:, :D], w_u[:, :, cols].reshape(D, 512))
            u = u + mm(x[:, D + RANK : D + 2 * RANK], u_b[pick[s], :, cols])
            gate[s, rows, cols] = g.astype(BF)
            up[s, rows, cols] = u.astype(BF)
            hidden[s, rows, cols] = (g * jax.nn.sigmoid(g) * u).astype(BF)

        grid_loop(2, 2, step)
        mid_s[s] = nb[s, :, :, :, D:].reshape(SPAN, EXT)

    def hid_back(s):
        def step(m, n):
            x = heads_of(cb, s, m)
            rows, cols = rows_of(m), cols_of(n)
            hb = mm(x[:, D : D + RANK], d_b[pick[s], :, cols])
            for z in range(4):
                hb = hb + mm_nt(x[:, z * 512 : (z + 1) * 512], w_d[z, cols, :])
            g = gate[s, rows, cols].astype(F32)
            u = up[s, rows, cols].astype(F32)
            sg = jax.nn.sigmoid(g)
            gate[s, rows, cols] = (hb * u * sg * (1.0 + g * (1.0 - sg))).astype(BF)
            up[s, rows, cols] = (hb * g * sg).astype(BF)

        grid_loop(2, 2, step)
        cot_s[s] = cb[s, :, :, :, D:].reshape(SPAN, EXT)

    def mid_back(s):
        def step(m, z):
            rows = rows_of(m)
            put_part(part1, s, m, z, mm_nt(gate[s, rows], w_g[z]) + mm_nt(up[s, rows], w_u[z]))

        grid_loop(2, 4, step)
        put_ext(part1, s, [mm_nt(gate[s], g_b[pick[s]]), mm_nt(up[s], u_b[pick[s]])])
        return Scatter(net, at, part1, s, set1, s_ids[s])

    def down(s):
        grid_loop(2, 4, lambda m, z: put_part(nb, s, m, z, mm(hidden[s, rows_of(m)], w_d[z])))
        put_ext(nb, s, [mm_nt(hidden[s], d_b[pick[s]])])

    def wide_terms(s):
        terms = [
            mm_tn(mid_s[s], gate[s])[:RANK],
            mm_tn(mid_s[s], up[s])[RANK : 2 * RANK],
            mm_tn(cot_s[s], hidden[s])[:RANK],
        ]
        for i, term in enumerate(terms):
            for j in range(4):
                vec1[3 + 4 * i + j, :, s * 256 : (s + 1) * 256] = term[
                    :, j * 256 : (j + 1) * 256
                ].astype(BF)

    def slices(full, i, s, term):
        for j in range(8):
            full[j, i, :, s * 256 : (s + 1) * 256] = term[:, j * 256 : (j + 1) * 256].astype(BF)

    def middle_back(s, t):
        pg, pu = t[:, D : D + RANK].astype(BF), t[:, D + RANK : D + 2 * RANK].astype(BF)
        back = t[:, :D] + mm(pg, gin[pick[s]]) + mm(pu, uin[pick[s]])
        mg = cot[s].astype(F32) + rms_back(midf[s], fgain[...], back)
        mgrad[s] = mg
        bg = mg.astype(BF)
        put_rows(cb, s, at, bg, [mm_nt(bg, aout[pick[s]])])
        gather = rows_gather(net, at, cb, s, n_ids[s])
        slices(full1, 0, s, mm_tn(pg, midn[s]))
        slices(full1, 1, s, mm_tn(pu, midn[s]))
        slices(full1, 2, s, mm_tn(inner_a[s].astype(BF), bg))
        return gather

    def attn_back(s):
        def step(m, unused):
            x = heads_of(cb, s, m)
            r = mm(x[:, D : D + RANK], a_b[pick[s]])
            for z in range(4):
                r = r + mm_nt(x[:, z * 512 : (z + 1) * 512], w_o[z])
            hidden[s, rows_of(m), 512:768] = r.astype(BF)

        grid_loop(2, 1, step)
        e = cb[s, :, :, :, D:].reshape(SPAN, EXT)
        vec1[15, :, s * 256 : (s + 1) * 256] = mm_tn(e, attn[s])[:RANK].astype(BF)

    def attend_back(s, g):
        if g == 0:
            dkv[...] = jnp.zeros(dkv.shape, F32)

        def step(m, unused):
            rows, keys = rows_of(m), keys_of(m)
            q, k = qb[s, g, rows], kvb[s, 0, keys]
            do = hidden[s, rows, 512 + g * 128 : 640 + g * 128]
            p = jnp.where(allowed(s, m), jnp.exp(mm_nt(q, k) - lse[s, g, rows]), 0.0)
            vg = mm_nt(do, kvb[s, 1, keys])
            delta = jnp.sum(p * vg, axis=-1, keepdims=True)
            sg = (p * (vg - delta)).astype(BF)
            dq = mm(sg, k) * SCALE
            hidden[s, rows, g * 128 : (g + 1) * 128] = (
                dq * cosb[s, rows] - pltpu.roll(dq, 64, 1) * sinb[s, rows]
            ).astype(BF)
            dkv[0, keys] += mm_tn(sg, q)
            dkv[1, keys] += mm_tn(p.astype(BF), do)

        grid_loop(2, 1, step)

    def halo_back(s):
        copies = []
        for hop in (2, 1, 0):
            for i in both:
                at_col = hop * 256 + i * 128
                gate[s, :, at_col : at_col + 128] = dkv[
                    i, (2 - hop) * SPAN : (3 - hop) * SPAN
                ].astype(BF)
            if hop > 0:
                copies.append(
                    net.push(
                        gate.at[s, :, pl.ds(hop * 256, 256)],
                        halo_in.at[s, hop - 1],
                        at.prev1 if hop == 1 else at.prev2,
                        halo_ids[4 + 2 * s + hop - 1],
                    )
                )
        return copies

    def qkv_back(s):
        def keys(m, unused):
            rows = rows_of(m)
            dk, dv = [
                gate[s, rows, i * 128 : (i + 1) * 128].astype(F32)
                + halo_in[s, 0, rows, i * 128 : (i + 1) * 128].astype(F32)
                + halo_in[s, 1, rows, i * 128 : (i + 1) * 128].astype(F32)
                for i in both
            ]
            hidden[s, rows, 256:384] = (
                dk * cosb[s, rows] - pltpu.roll(dk, 64, 1) * sinb[s, rows]
            ).astype(BF)
            hidden[s, rows, 384:512] = dv.astype(BF)

        grid_loop(2, 1, keys)
        raw = hidden[s, :, :512]
        px[s] = jnp.zeros(px.shape[1:], BF)
        px[s, :, :, :RANK] = mm_nt(raw, q_b[pick[s]]).astype(BF).reshape(8, TOK, RANK)
        pairs = []
        for k in range(1, 8):
            peer = (h + k) % 8
            pairs.append((px.at[s, peer], px_in.at[s, k - 1], (peer, b)))
        exchange = net.spread(pairs, px_in.at[s], px_ids[s])
        grid_loop(
            2, 4, lambda m, z: put_part(part1, s, m, z, mm_nt(hidden[s, rows_of(m), :512], w_q[z]))
        )
        scatter = Scatter(net, at, part1, s, set1, s_ids[s])
        term = mm_tn(next_s[s], raw)[:RANK]
        for j in range(4):
            vec2[s * 8 + 4 + j] = term[:, j * 128 : (j + 1) * 128].astype(BF)
        return scatter, exchange

    def finish_result(s, t):
        inn = t[:, D : D + RANK].astype(BF)
        midf[s] = midf[s] + t[:, :D] + mm(inn, dout[pick[s]])
        slices(full2, 1, s, mm_tn(inn, cot[s]))

    def p_sum(s, exchange):
        exchange.wait_recv()
        total = px[s, h].astype(F32)
        for k in range(7):
            total = total + px_in[s, k].astype(F32)
        p = total[:, :RANK].astype(BF)
        slices(full2, 0, s, mm_tn(p, normed[s]))
        return p

    def finish_grad(s, t, p):
        back = t[:, :D] + mm(p, qin[pick[s]])
        mgrad[s] = mgrad[s] + rms_back(tok[s].astype(F32), again[...], back)

    loads[0].wait()
    loads[1].wait()
    W_Q.step(1)
    W_O.step(1)
    norm_in(0)
    n0 = rows_gather(net, at, nb, 0, n_ids[0])
    for copy in loads[2:5]:
        copy.wait()
    W_G.step(1)
    W_Q.step(2)
    W_O.step(2)
    norm_in(1)
    grid_loop(2, 8, table)
    W_Q.step(3)
    n0.relay()
    n1 = rows_gather(net, at, nb, 1, n_ids[1])
    W_G.step(2)
    W_U.step(1)
    W_O.step(3)
    cot_in(0)
    cot_in(1)
    n0.last()
    n1.relay()
    c0 = rows_gather(net, at, cb, 0, c_ids[0])
    W_Q.step(4)
    W_G.step(3)
    for copy in loads[5:]:
        copy.wait()
    n0.done()
    W_Q.step(5)
    qkv(0)
    halo0 = halo(0)
    W_O.step(4)
    W_U.step(2)
    W_D.step(1)
    n1.last()
    c0.relay()
    c1 = rows_gather(net, at, cb, 1, c_ids[1])
    n1.done()
    qkv(1)
    halo1 = halo(1)
    W_U.step(3)
    W_D.step(2)
    n0.settle()
    n1.settle()
    c0.last()
    W_O.step(5)
    W_G.step(4)
    for copy in halo0:
        copy.wait_recv()
    attend(0, 0)
    c1.relay()
    attend(0, 1)
    s0 = out_proj(0)
    c1.last()
    for copy in halo1:
        copy.wait_recv()
    attend(1, 0)
    s0.merge()
    attend(1, 1)
    s1 = out_proj(1)
    s0.relay()
    W_D.step(3)
    s1.merge()
    m0 = middle(0, s0.done())
    s1.relay()
    W_U.step(4)
    m0.relay()
    c0.done()
    c1.done()
    m1 = middle(1, s1.done())
    W_G.step(5)
    m0.last()
    m1.relay()
    W_D.step(4)
    m0.done()
    m1.last()
    W_U.step(5)
    ffn(0)
    m1.done()
    ffn(1)
    W_D.step(5)
    for item in (c0, c1, m0, m1, W_Q, W_G, W_U):
        item.settle()
    hid_back(0)
    s0 = mid_back(0)
    hid_back(1)
    s0.merge()
    s1 = mid_back(1)
    s0.relay()
    down(0)
    s1.merge()
    down(1)
    b0 = middle_back(0, s0.done())
    s1.relay()
    wide_terms(0)
    wide_terms(1)
    b0.relay()
    b1 = middle_back(1, s1.done())
    fold1.heads()
    b0.last()
    r0 = Scatter(net, at, nb, 0, set2, t_ids[0])
    r1 = Scatter(net, at, nb, 1, set2, t_ids[1])
    b0.done()
    attn_back(0)
    attend_back(0, 0)
    b1.relay()
    attend_back(0, 1)
    back0 = halo_back(0)
    b1.last()
    vec1[0:3] = fold1.heads_sum().astype(BF)
    b1.done()
    attn_back(1)
    fold1.blocks()
    r0.merge()
    r1.merge()
    attend_back(1, 0)
    fold1.blocks_sum()
    r0.relay()
    attend_back(1, 1)
    back1 = halo_back(1)
    b0.settle()
    b1.settle()
    for copy in back0:
        copy.wait_recv()
    s0, x0 = qkv_back(0)
    r1.relay()
    fold1.near_done()
    spread = Weight(net, at, out1, True, q_ids)
    spread.step(1)
    s0.merge()
    finish_result(0, r0.done())
    for copy in back1:
        copy.wait_recv()
    s1, x1 = qkv_back(1)
    spread.step(2)
    s0.relay()
    s1.merge()
    finish_result(1, r1.done())
    p0 = p_sum(0, x0)
    p1 = p_sum(1, x1)
    fold2.heads()
    spread.step(3)
    s1.relay()
    total = fold2.heads_sum()
    for i in both:
        for s in both:
            for j in both:
                vec2[s * 8 + 2 * i + j] = total[
                    i, :, s * 256 + j * 128 : s * 256 + (j + 1) * 128
                ].astype(BF)
    fold2.blocks()
    finish_grad(0, s0.done(), p0)
    spread.step(4)
    fold2.blocks_sum()
    finish_grad(1, s1.done(), p1)
    fold2.near_done()
    fold2.far((c_ids[0] + c_ids[1])[:15])
    spread.step(5)
    writes = [
        pltpu.make_async_copy(midf, result_o, local.at[0]),
        pltpu.make_async_copy(mgrad, igrad_o, local.at[1]),
        pltpu.make_async_copy(out1, sums1_o, local.at[2]),
    ]
    for copy in writes:
        copy.start()
    fold2.far_done()
    writes.append(pltpu.make_async_copy(out2, sums2_o, local.at[3]))
    writes[3].start()
    net.drain()
    for copy in writes:
        copy.wait()


def call_layer(args):
    vm = lambda *shape, t=BF: pltpu.VMEM(shape, t)
    rs = lambda: [vm(2, TOK // 2, CW), vm(2, TOK // 2, CW), vm(2, TOK, CW), vm(2, TOK, CW)]
    outs = [((2, TOK, D), F32), ((2, TOK, D), F32), ((4, 512, 512), BF), ((4, 512, 128), BF)]
    scratch = (
        [vm(4, 512, 512), vm(4, 256, 512), vm(4, 512, 1024), vm(4, 512, 1024), vm(4, 1024, 512)]
        + [vm(2, 4, 2, TOK, CW)] * 3
        + [vm(2, 4, TOK, D + EXT), vm(2, 4, TOK, D + EXT)]
        + rs() + rs()
        + [vm(2, SPAN, 1024)] * 3
        + [vm(2, 2, SPAN, 128), vm(2, 2, 1536, 128), vm(2, SPAN, 256), vm(2, 2, SPAN, 1, t=F32)]
        + [vm(2, SPAN, 128, t=F32)] * 2
        + [vm(2, SPAN, 1, t=jnp.int32)]
        + [vm(2, TOK, D, t=F32), vm(2, TOK, D), vm(2, TOK, D), vm(2, TOK, RANK, t=F32)]
        + [vm(2, TOK, D, t=F32)] + [vm(2, SPAN, EXT)] * 3
        + [vm(2, 1536, 128, t=F32), vm(2, 2, SPAN, 256)]
        + [vm(2, RANK, 256), vm(2, RANK, 1024), vm(2, RANK, 512), vm(2, RANK, 1024), vm(2, RANK, 1024)]
        + [vm(8, 3, RANK, 512), vm(7, 3, RANK, 512), vm(16, RANK, 512), vm(15, RANK, 512)]
        + [vm(8, 2, RANK, 512), vm(7, 2, RANK, 512), vm(16, RANK, 128), vm(15, RANK, 128)]
        + [vm(2, 8, TOK, EXT), vm(2, 7, TOK, EXT)]
        + [pltpu.SemaphoreType.DMA((N_SEMS,)), pltpu.SemaphoreType.DMA((N_SEMS,)), pltpu.SemaphoreType.DMA((10,))]
    )
    smem = pl.BlockSpec(memory_space=pltpu.SMEM)
    vmem = pl.BlockSpec(memory_space=pltpu.VMEM)
    hbm = pl.BlockSpec(memory_space=pl.ANY)
    return pl.pallas_call(
        layer,
        out_shape=[jax.ShapeDtypeStruct(shape, kind) for shape, kind in outs],
        in_specs=[smem] * 2 + [vmem] * 5 + [hbm] * 5 + [vmem] * 5 + [hbm] * 5,
        out_specs=[hbm] * len(outs),
        scratch_shapes=scratch,
        compiler_params=pltpu.CompilerParams(
            collective_id=0, has_side_effects=True, vmem_limit_bytes=VMEM_BYTES
        ),
    )(*args)


def unpack(
    index_ref, result, igrad, sums1, sums2,
    result_o, igrad_o, qi_o, qo_o, ai_o, ao_o, gi_o, go_o, ui_o, uo_o, di_o, do_o, sem,
):
    copies = [
        pltpu.make_async_copy(result, result_o, sem.at[0]),
        pltpu.make_async_copy(igrad, igrad_o, sem.at[1]),
    ]
    for copy in copies:
        copy.start()
    swap = index_ref[0] == 1

    def emit(out, cols, first, second):
        first, second = first.astype(F32), second.astype(F32)
        out[0, :, cols] = jnp.where(swap, second, first)
        out[1, :, cols] = jnp.where(swap, first, second)

    def found(ref, j, head, width):
        row0 = (j % 4) * 128 + head * RANK
        return ref[j // 4, row0 : row0 + RANK, :width]

    for head in range(8):
        for j, out in ((0, gi_o), (1, ui_o), (2, ao_o), (15, ai_o)):
            block = found(sums1, j, head, 512)
            emit(out, pl.ds(head * 256, 256), block[:, :256], block[:, 256:])
        for i, out in enumerate([go_o, uo_o, di_o]):
            for k in range(4):
                block = found(sums1, 3 + 4 * i + k, head, 512)
                emit(out, pl.ds(head * 1024 + k * 256, 256), block[:, :256], block[:, 256:])
        for j, out, width in (
            (0, qi_o, 256), (1, qi_o, 256), (2, do_o, 256), (3, do_o, 256),
            (4, qo_o, 512), (5, qo_o, 512), (6, qo_o, 512), (7, qo_o, 512),
        ):
            cols = pl.ds(head * width + (j % (width // 128)) * 128, 128)
            emit(out, cols, found(sums2, j, head, 128), found(sums2, 8 + j, head, 128))
    for copy in copies:
        copy.wait()


def call_unpack(index, arrays):
    narrow, wide = (2, RANK, D), (2, RANK, 8192)
    outs = [
        (2, TOK, D), (2, TOK, D), narrow, (2, RANK, 4096), narrow, narrow,
        narrow, wide, narrow, wide, wide, narrow,
    ]
    smem = pl.BlockSpec(memory_space=pltpu.SMEM)
    vmem = pl.BlockSpec(memory_space=pltpu.VMEM)
    hbm = pl.BlockSpec(memory_space=pl.ANY)
    return pl.pallas_call(
        unpack,
        out_shape=[jax.ShapeDtypeStruct(shape, F32) for shape in outs],
        in_specs=[smem] + [vmem] * 4,
        out_specs=[hbm, hbm] + [vmem] * 10,
        scratch_shapes=[pltpu.SemaphoreType.DMA((2,))],
        compiler_params=pltpu.CompilerParams(vmem_limit_bytes=VMEM_BYTES),
    )(index, *arrays)


def body(
    tokens, cotangent, doc_lengths, adapter_index, attn_gain, ffn_gain,
    w_qkv, w_out, w_gate, w_up, w_down,
    qkv_in, qkv_out, attn_in, attn_out, gate_in, gate_out, up_in, up_out, down_in, down_out,
):
    flip = lambda g: jnp.swapaxes(g, 1, 2)
    half = np.arange(64, dtype=np.float32) * np.float32(2.0 / 128)
    inverse = np.power(np.float32(THETA), -half).astype(np.float32)
    inv = jnp.asarray(np.concatenate([inverse, inverse])[None])
    index = adapter_index.reshape(2)
    arrays = call_layer((
        index, doc_lengths, tokens, cotangent, attn_gain[None], ffn_gain[None], inv,
        w_qkv, w_out, w_gate, w_up, w_down,
        flip(qkv_in), flip(gate_in), flip(up_in), attn_out, down_out, flip(attn_in), flip(down_in),
        qkv_out, gate_out, up_out,
    ))
    result, igrad, qi, qo, ai, ao, gi, go, ui, uo, di, do = call_unpack(index, arrays)
    return (
        result, igrad, flip(qi), qo, flip(ai), ao, flip(gi), go, flip(ui), uo, flip(di), do
    )


def solution(mesh):
    row = P(None, ("blk", "head"), None)
    return jax.shard_map(
        body,
        mesh=mesh,
        in_specs=(row, row) + (P(),) * 4
        + (P("blk", "head"), P("head", "blk"), P("blk", "head"), P("blk", "head"), P("head", "blk"))
        + (P(),) * 10,
        out_specs=(row, row) + (P(),) * 10,
        check_vma=False,
    )
```

time: 320 us -> 268 us (0.84)
  Pallas kernels: 305 us -> 267 us
  local copies, waits for them, and re-layouts: 13.7 us -> 0 us
    pallas_call x1, Pallas kernels: 305 us -> 261 us  [call_layer(): pl.pallas_call(layer, out_shape=[jax.ShapeDtypeStruct(shape, kind) for sh...]
    unnamed x37 -> x0, local copies, waits for them, and re-layouts: 13.7 us -> none
    pallas_call x0 -> x1, Pallas kernels: none -> 6 us  [call_unpack(): pl.pallas_call(unpack, out_shape=[jax.ShapeDtypeStruct(shape, F32) for sh...]
where the time goes in v1:
time: 268 us; the launch traced here: 267 us
  Pallas kernels  267 us (100%)
    pallas_call x1, Pallas kernels, call_layer(): pl.pallas_call(layer, out_shape=[jax.ShapeDtypeStruct(shape, kind) for sh...  261 us
    pallas_call x1, Pallas kernels, call_unpack(): pl.pallas_call(unpack, out_shape=[jax.ShapeDtypeStruct(shape, F32) for sh...  6 us

profile of v1, /device:TPU:1, one launch (start us, length us, event | category | flops | bytes accessed | tf_op | source)
XLA Modules:
  0.0 267.4 jit_solution(14822496680422903649)
XLA Ops:
  0.7 260.5 %shard_map.301 = (f32[2,64,2048]{2,1,0:T(8,128)}, f32[2,64,2048]{2,1,0:T(8,128)}, bf16[4,512,512]{2,1,0:T(8,128)(2,1)}, bf16[4,512,128]{2,1,0:T(8,128)(2,1)}) custom-call(s32[2]{0:T(128)} %bitcast.20, s32[2,4]{1,0:T(2,128)} %length_ref.1, bf16[2,64,2048]{2,1,0:T(8,128)(2,1)} %tok.1, bf16[2,64,2048]{2,1,0:T(8,128)(2,1)} %cot.1, f32[1,2048]{1,0:T(1,128)} %bitcast.18, ...), custom_call_target="tpu_custom_call" | custom-call | tf_op jit(solution)/shard_map/pallas_call | solution.py:914
  261.2 6.0 %shard_map.302 = (f32[2,64,2048]{2,1,0:T(8,128)}, f32[2,64,2048]{2,1,0:T(8,128)}, f32[2,16,2048]{2,1,0:T(8,128)}, f32[2,16,4096]{2,1,0:T(8,128)}, f32[2,16,2048]...) custom-call(s32[2]{0:T(128)} %bitcast.21, ...), custom_call_target="tpu_custom_call" | custom-call | tf_op jit(solution)/shard_map/pallas_call | solution.py:974
